TPU v7x, 512 devices: a whole 4x4x16 slice. The times are simulated.
512 devices in a mesh: row: 16 (over z), col: 32 (over y, x, core).
Axes of the slice: x: 4, y: 4, z: 16, core: 2. Of those that a mesh axis runs over, the one named last changes fastest.
Arguments:
- weight: bfloat16 [8192, 28672], P('row', 'col'), may hold values from -3 to 3
- gradient: bfloat16 [8192, 28672], P('row', 'col'), may hold values from -6 to 6
- momentum: bfloat16 [8192, 28672], P('row', 'col'), may hold values from -6 to 6
- basis: bfloat16 [28672, 512], P('col', 'row'), may hold values from -6 to 6
Outputs:
- new_weight: bfloat16 [8192, 28672], P('row', 'col')
- new_momentum: bfloat16 [8192, 28672], P('row', 'col')
- new_basis: bfloat16 [28672, 512], P('col', 'row')
All inputs are finite; a program needn't handle non-finite values.
Results may differ from a plain program's by a relative error of at most 0.012.
Values may be sent and summed in bfloat16 or wider, within the bound.
A program may use at most 64 MiB of HBM per device.

v0:
```python
import math

import jax
import jax.numpy as jnp
from jax import lax
from jax.sharding import PartitionSpec as P

D = 8192
FF = 28672
RANK = 512


def solve_right(factor, values):
    return lax.linalg.triangular_solve(
        factor, values, left_side=False, lower=True, transpose_a=True
    )


def squares(values):
    return jnp.sum(values * values, axis=0)


def local(weight, gradient, momentum, basis):
    buffer = (momentum.astype(jnp.float32) + gradient.astype(jnp.float32)).astype(jnp.bfloat16)
    partial_left = jnp.dot(
        buffer, lax.all_gather(basis, "row", axis=1, tiled=True), preferred_element_type=jnp.float32
    )
    left = lax.psum(partial_left, "col").astype(jnp.bfloat16)
    gram_part = lax.dot_general(
        left, left, (((0,), (0,)), ((), ())), preferred_element_type=jnp.float32
    )
    cross_part = lax.dot_general(
        buffer, left, (((0,), (0,)), ((), ())), preferred_element_type=jnp.float32
    )
    gram = lax.psum(gram_part, "row")
    factor = jnp.linalg.cholesky(gram)
    cross = lax.psum(cross_part, "row")
    right = solve_right(factor, cross)
    totals = lax.psum(squares(right), "col")
    scale = lax.rsqrt(totals / FF + 1e-06)
    new_full = (right * scale[None, :]).astype(jnp.bfloat16)
    rank_dev = basis.shape[1]
    new_basis = lax.dynamic_slice_in_dim(new_full, lax.axis_index("row") * rank_dev, rank_dev, 1)
    ortho = solve_right(factor, left.astype(jnp.float32))
    correction = lax.dot_general(
        ortho, right, (((1,), (1,)), ((), ())), precision=lax.Precision.HIGHEST
    )
    new_momentum = (buffer.astype(jnp.float32) - 0.2 * correction).astype(jnp.bfloat16)
    update = lax.dot_general(
        ortho.astype(jnp.bfloat16),
        new_full,
        (((1,), (1,)), ((), ())),
        preferred_element_type=jnp.float32,
    )
    new_weight = (weight.astype(jnp.float32) - 0.5 * math.sqrt(D / RANK) * update).astype(
        jnp.bfloat16
    )
    return (new_weight, new_momentum, new_basis)


def solution(mesh):
    return jax.shard_map(
        local,
        mesh=mesh,
        in_specs=(P("row", "col"), P("row", "col"), P("row", "col"), P("col", "row")),
        out_specs=(P("row", "col"), P("row", "col"), P("col", "row")),
        check_vma=False,
    )
```

profile of v0, /device:TPU:1, one launch (start us, length us, event | category | flops | bytes accessed | tf_op | source)
XLA Modules:
  0.0 559.1 jit_solution(8508334422733079150)
XLA Ops:
  7.2 34.9 %all_gather.3 = bf16[896,512]{0,1:T(8,128)(2,1)S(1)} all-gather(bf16[896,32]{0,1:T(8,128)(2,1)} %param.7), channel_id=1, replica_groups=mesh['row'=16,'col'=32] {'row'}, dimensions={1}, use_global_device_ids=true | all-gather | bytes 974848 | tf_op jit(solution)/shard_map/all_gather | solution.py:26
  42.1 2.3 fusion.57
  44.4 136.2 %all-reduce.6 = bf16[512,512]{1,0:T(8,128)(2,1)S(1)} all-reduce(f32[512,512]{1,0:T(8,128)S(1)} %fusion.57), channel_id=1, replica_groups=mesh['row'=16,'col'=32] {'col'}, use_global_device_ids=true, to_apply=%region_0.0 | all-reduce | flops 262144 | bytes 1572864 | tf_op jit(solution)/shard_map/psum | solution.py:28
  180.6 1.9 fusion.56
  182.6 1.5 fusion.59
  184.1 1.1 convert_element_type.38
  185.2 135.6 %all-reduce.5.cloned.1.call-done = (f32[896,512]{1,0:T(8,128)}, f32[512,512]{0,1:T(8,128)}) async-done(((f32[896,512]{1,0:T(8,128)}, f32[512,512]{0,1:T(8,128)}), (f32[896,512]{1,0:T(8,128)}, f32[512,512]{0,1:T(8,128)})) %all-reduce.5.cloned.1.call-update) | async-done | bytes 2883600 | tf_op jit(solution)/shard_map/psum | solution.py:37
  320.8 1.6 copy.8
  322.5 0.2 fusion.9
  322.7 1.0 copy-done.2
  323.7 11.7 %cholesky.104 = f32[128,128]{1,0:T(8,128)S(1)} custom-call(f32[128,128]{1,0:T(8,128)S(1)} %cholesky.266), custom_call_target="Cholesky" | custom-call | tf_op jit(solution)/shard_map/jit(cholesky)/cholesky | solution.py:36
  335.5 9.8 %custom-call.32 = f32[1,128,128]{1,2,0:T(8,128)S(1)} custom-call(f32[1,128,128]{2,1,0:T(8,128)S(1)} %get-tuple-element.32), custom_call_target="InvertDiagBlocksLowerTriangular" | custom-call | tf_op jit(solution)/shard_map/jit(cholesky)/cholesky | solution.py:36
  345.3 0.1 cholesky.224
  345.4 1.2 constant_dynamic-update-slice_fusion.3
  346.6 1.3 convolution_subtract_fusion.5
  347.9 11.7 %cholesky.217 = f32[128,128]{1,0:T(8,128)S(1)} custom-call(f32[128,128]{1,0:T(8,128)S(1)} %cholesky.270), custom_call_target="Cholesky" | custom-call | tf_op jit(solution)/shard_map/jit(cholesky)/cholesky | solution.py:36
  359.7 9.9 %custom-call.33 = f32[1,128,128]{1,2,0:T(8,128)S(1)} custom-call(f32[1,128,128]{2,1,0:T(8,128)S(1)} %get-tuple-element.29), custom_call_target="InvertDiagBlocksLowerTriangular" | custom-call | tf_op jit(solution)/shard_map/jit(cholesky)/cholesky | solution.py:36
  369.6 0.3 convolution_dynamic-update-slice_fusion
  369.9 1.3 convolution_subtract_fusion.6
  371.2 11.7 %cholesky.238 = f32[128,128]{1,0:T(8,128)S(1)} custom-call(f32[128,128]{1,0:T(8,128)S(1)} %cholesky.275), custom_call_target="Cholesky" | custom-call | tf_op jit(solution)/shard_map/jit(cholesky)/cholesky | solution.py:36
  382.9 0.7 compare_reduce_fusion.1
  383.7 9.8 %custom-call.34 = f32[1,128,128]{1,2,0:T(8,128)S(1)} custom-call(f32[1,128,128]{2,1,0:T(8,128)S(1)} %get-tuple-element.26), custom_call_target="InvertDiagBlocksLowerTriangular" | custom-call | tf_op jit(solution)/shard_map/jit(cholesky)/cholesky | solution.py:36
  393.5 0.2 convolution_dynamic-update-slice_fusion.1
  393.7 1.2 convolution_subtract_fusion.7
  394.9 11.9 %cholesky.255 = f32[128,128]{1,0:T(8,128)S(1)} custom-call(f32[128,128]{1,0:T(8,128)S(1)} %convolution_subtract_fusion.7), custom_call_target="Cholesky" | custom-call | tf_op jit(solution)/shard_map/jit(cholesky)/cholesky | solution.py:36
  406.9 0.6 compare_reduce_fusion
  407.5 0.6 compare_reduce_fusion.2
  410.7 0.1 select_select_fusion
  410.8 8.0 %while.1 = (s32[]{:T(128)}, f32[512,512]{1,0:T(8,128)S(1)}, s32[4,2]{0,1:T(2,128)S(1)}, f32[4,128,128]{2,1,0:T(8,128)S(1)}, s32[]{:T(128)}) while((s32[]{:T(128)}, f32[512,512]{1,0:T(8,128)S(1)}, s32[4,2]{0,1:T(2,128)S(1)}, f32[4,128,128]{2,1,0:T(8,128)S(1)}, s32[]{:T(128)}) %tuple.31), condition=%wide.while_cond, body=%wide.while_body.sunk | while | flops 2 | bytes 131181 | solution.py:14
  410.8 0.1 constant_dynamic-slice_fusion.3
  410.9 0.5 fusion.75
  411.4 1.4 bitcast_dynamic-update-slice_fusion.2
  412.8 0.1 constant_dynamic-slice_fusion.3
  412.9 0.5 fusion.75
  413.4 1.4 bitcast_dynamic-update-slice_fusion.2
  414.8 0.1 constant_dynamic-slice_fusion.3
  414.9 0.5 fusion.75
  415.4 1.4 bitcast_dynamic-update-slice_fusion.2
  416.9 0.5 fusion.75
  417.4 1.4 bitcast_dynamic-update-slice_fusion.2
  418.8 39.3 %custom-call.35 = f32[4,128,128]{1,2,0:T(8,128)S(1)} custom-call(f32[4,128,128]{2,1,0:T(8,128)S(1)} %get-tuple-element.10), custom_call_target="InvertDiagBlocksLowerTriangular" | custom-call | tf_op jit(solution)/shard_map/triangular_solve | solution.py:14
  458.2 0.3 fusion.33
  458.5 1.5 convolution_subtract_fusion.3
  460.0 0.4 fusion.43
  460.5 1.0 convolution_subtract_fusion.2
  461.5 0.4 fusion.45
  461.9 1.5 convolution_subtract_fusion.4
  463.4 0.4 fusion.47
  463.8 0.6 fusion.23
  464.4 0.9 convolution_subtract_fusion.1
  465.3 0.6 fusion.42
  466.0 1.6 convolution_subtract_fusion
  467.6 0.6 fusion.44
  468.2 2.4 fusion.6
  470.6 0.6 fusion.46
  471.2 0.2 multiply_reduce_fusion
  471.4 0.3 copy-done.7
  471.8 0.3 copy-done.9
  472.0 4.8 subtract_convert_fusion
  476.9 71.5 %psum.31 = f32[512]{0:T(512)S(1)} all-reduce(f32[512]{0:T(512)S(1)} %multiply_reduce_fusion), channel_id=1, replica_groups=mesh['row'=16,'col'=32] {'col'}, use_global_device_ids=true, to_apply=%region_12.13 | all-reduce | flops 512 | bytes 4096 | tf_op jit(solution)/shard_map/psum | solution.py:39
  548.4 0.2 multiply_convert_fusion
  548.6 1.0 copy-done.12
  549.5 1.7 subtract_convert_fusion.1
  551.2 0.6 constant_dynamic-slice_fusion.1
  (36 shorter events, 0.4 us)
Async XLA Ops:
  7.2 313.7 %all-reduce.5.cloned.1.call-start = ((), (), s32[]{:S(2)}) async-start(), calls=%async_computation | async-start | bytes 5767168 | tf_op jit(solution)/shard_map/psum | solution.py:37
  42.1 138.6 %copy-start.6 = (bf16[512,896]{1,0:T(8,128)(2,1)S(1)}, bf16[512,896]{1,0:T(8,128)(2,1)}, u32[]{:S(2)}) copy-start(bf16[512,896]{1,0:T(8,128)(2,1)} %param.5) | copy-start | bytes 2752516
  42.1 138.6 %copy-start.8 = (bf16[512,896]{1,0:T(8,128)(2,1)S(1)}, bf16[512,896]{1,0:T(8,128)(2,1)}, u32[]{:S(2)}) copy-start(bf16[512,896]{1,0:T(8,128)(2,1)} %param.6) | copy-start | bytes 2752516
  320.8 1.7 copy-start
  322.7 1.0 copy-start.2
  410.8 49.7 %copy-start.1 = (f32[512,512]{1,0:T(8,128)S(1)}, f32[512,512]{1,0:T(8,128)}, u32[]{:S(2)}) copy-start(f32[512,512]{1,0:T(8,128)} %convert_element_type.38) | copy-start | bytes 3145732
  458.2 7.2 %copy-start.4 = (f32[4,128,128]{1,2,0:T(8,128)}, f32[4,128,128]{1,2,0:T(8,128)S(1)}, u32[]{:S(2)}) copy-start(f32[4,128,128]{1,2,0:T(8,128)S(1)} %custom-call.35) | copy-start | bytes 786436
  460.5 3.3 copy-start.3
  463.8 7.7 %copy-start.10 = (f32[512,128]{0,1:T(8,128)}, f32[512,128]{0,1:T(8,128)S(1)}, u32[]{:S(2)}) copy-start(f32[512,128]{0,1:T(8,128)S(1)} %fusion.47) | copy-start | bytes 786436
  466.0 1.6 copy-start.5
  470.6 1.2 copy-start.7
  470.6 1.4 copy-start.9
  476.9 71.7 %copy-start.11 = (f32[512,128]{0,1:T(8,128)S(1)}, f32[512,128]{0,1:T(8,128)}, u32[]{:S(2)}) copy-start(f32[512,128]{0,1:T(8,128)} %copy-done.10) | copy-start | bytes 786436
  548.3 1.2 copy-start.12
Sparse Core Ops, SparseCore 0:
  184.2 136.5 all-reduce.4
where the time goes:
time: 569 us; the launch traced here: 559 us
  blocking collectives  243 us (43%)
  waiting for transfers between devices  136 us (24%)
  other arithmetic  120 us (21%)
  matrix products  30.6 us (5%)
  between operations  17.4 us (3%)
  local copies, waits for them, and re-layouts  12.9 us (2%)
    psum x1, blocking collectives, local(): left = lax.psum(partial_left, 'col').astype(jnp.bfloat16)  136 us
    psum x1, waiting for transfers between devices, local(): cross = lax.psum(cross_part, 'row')  136 us
    another operation x14, other arithmetic, local(): factor = jnp.linalg.cholesky(gram)  78.7 us
    psum x1, blocking collectives, local(): totals = lax.psum(squares(right), 'col')  71.5 us
    another operation x3, other arithmetic, solve_right(): lax.linalg.triangular_solve(factor, values, left_side=False, lower=True,...  39.4 us
    all_gather x1, blocking collectives, local(): lax.all_gather(basis, 'row', axis=1, tiled=True)  34.9 us
    another operation x14, matrix products, solve_right(): lax.linalg.triangular_solve(factor, values, left_side=False, lower=True,...  12.9 us
  transfers between devices with their start and end apart: 1, of which 1 were waited for; matrix products, arithmetic and copies ran while one was open for 0% of the time, Pallas kernels for 0%

commit v1 on v0

v1 whole, which is shorter than its diff:
```python
import math

import jax
import jax.numpy as jnp
from jax import lax
from jax.experimental import pallas as pl
from jax.experimental.pallas import tpu as pltpu
from jax.sharding import PartitionSpec as P

D = 8192
FF = 28672
RANK = 512
ROWS = 16
COLS = 32
TILES = 5
F32 = jnp.float32
BF16 = jnp.bfloat16
HIGHEST = lax.Precision.HIGHEST
MESH = pl.DeviceIdType.MESH
VMEM = pl.BlockSpec(memory_space=pltpu.VMEM)
ANY = pl.BlockSpec(memory_space=pl.ANY)
DMA = pltpu.SemaphoreType.DMA
NN = (((1,), (0,)), ((), ()))
NT = (((1,), (1,)), ((), ()))
TN = (((0,), (0,)), ((), ()))


def remote(src, dst, send, recv, **where):
    return pltpu.make_async_remote_copy(
        src_ref=src, dst_ref=dst, send_sem=send, recv_sem=recv, device_id=where, device_id_type=MESH)


def wait_bytes(ref, sem):
    pltpu.make_async_copy(ref, ref, sem).wait()


def ring(a):
    return lax.rem(a + 2 * ROWS, ROWS)


def greet(r, c):
    barrier = pltpu.get_barrier_semaphore()
    for k in (1, 2, ROWS - 1, ROWS - 2):
        pl.semaphore_signal(barrier, inc=1, device_id={"row": ring(r + k)}, device_id_type=MESH)

    def one(k, carry):
        pl.semaphore_signal(barrier, inc=1, device_id={"col": lax.rem(c + k, COLS)}, device_id_type=MESH)
        return carry

    lax.fori_loop(1, COLS, one, 0)
    return barrier, 4 + COLS - 1


def col_send(c, src_of, dst, send, recv):
    def one(k, carry):
        d = lax.rem(c + k, COLS)
        remote(src_of(d), dst, send, recv, col=d).start()
        return carry

    lax.fori_loop(1, COLS, one, 0)


class Gather:
    def __init__(self, r, buf, send, recv):
        self.r, self.buf, self.send, self.recv = r, buf, send, recv

    def message(self, way, d):
        sign = 1 if way == 0 else -1
        step = jnp.minimum(d, 2)
        block = self.buf.at[ring(self.r - sign * (d - step))]
        return remote(block, block, self.send.at[way, d], self.recv.at[way, d], row=ring(self.r + sign * step))

    def start(self):
        for d in (2, 1):
            for way in range(2):
                self.message(way, d).start()

    def forward(self, d):
        for way in range(2):
            self.message(way, d).wait_recv()
            last = 8 - way

            @pl.when(d + 2 <= last)
            def _():
                self.message(way, d + 2).start()

    def end(self, d):
        self.message(0, d).wait_recv()

        @pl.when(d <= 7)
        def _():
            self.message(1, d).wait_recv()

    def drain(self):
        def one(d, carry):
            self.message(0, d).wait_send()

            @pl.when(d <= 7)
            def _():
                self.message(1, d).wait_send()

            return carry

        lax.fori_loop(1, 9, one, 0)


class Reduce:
    def __init__(self, r, part, slots, first, send, recv):
        self.r, self.part, self.slots, self.first, self.send, self.recv = r, part, slots, first, send, recv
        self.size = RANK // ROWS

    def own(self, block):
        return self.part[pl.ds(pl.multiple_of(block * self.size, self.size), self.size), :]

    def message(self, way, d, src):
        sign = 1 if way == 0 else -1
        return remote(
            src, self.slots.at[way, d], self.send.at[way, d], self.recv.at[way, d],
            row=ring(self.r + sign * jnp.minimum(d, 2)))

    def start(self):
        for i in range(2):
            for way in range(2):
                d = 8 - way - i
                here = self.first.at[way, i]
                here[...] = self.own(ring(self.r + (d if way == 0 else -d))).astype(BF16)
                self.message(way, d, here).start()

    def forward(self, k):
        for way in range(2):
            def go():
                d = 6 - way - k
                got = self.slots.at[way, d + 2]
                self.message(way, d + 2, got).wait_recv()
                got[...] = (got[...].astype(F32) + self.own(ring(self.r + (d if way == 0 else -d)))).astype(BF16)
                self.message(way, d, got).start()

            if way == 0:
                go()
            else:
                pl.when(k < 5)(go)

    def end(self):
        total = self.own(self.r)
        for way in range(2):
            for d in (2, 1):
                self.message(way, d, self.first.at[0, 0]).wait_recv()
                total = total + self.slots[way, d].astype(F32)
        return total

    def drain(self):
        def one(d, carry):
            self.message(0, d, self.first.at[0, 0]).wait_send()

            @pl.when(d <= 7)
            def _():
                self.message(1, d, self.first.at[0, 0]).wait_send()

            return carry

        lax.fori_loop(1, 9, one, 0)


def split(x):
    high = x.astype(BF16)
    return high, (x - high.astype(F32)).astype(BF16)


def factor_block(w):
    sub = lax.broadcasted_iota(jnp.int32, (8, 256), 0)

    def twice(x):
        return jnp.concatenate([x, x], axis=1)

    for p in range(16):
        panel = w[p]
        columns = [jnp.broadcast_to(panel[:, 8 * p + j:8 * p + j + 1], (8, 128)) for j in range(8)]
        s = {}
        for j in range(8):
            for i in range(j + 1):
                s[i, j] = jnp.broadcast_to(columns[j][i:i + 1, :], (8, 128))
        rows = [jnp.broadcast_to(panel[k:k + 1, :], (8, 256)) for k in range(8)]
        for j in range(8):
            root = lax.rsqrt(s[j, j])
            u = {i: s[j, i] * root for i in range(j + 1, 8)}
            for i in range(j + 1, 8):
                for l in range(i, 8):
                    s[i, l] = s[i, l] - u[i] * u[l]
            rows[j] = rows[j] * twice(root)
            for i in range(j + 1, 8):
                rows[i] = rows[i] - twice(u[i]) * rows[j]
        done = rows[7]
        for k in range(7):
            done = jnp.where(sub == k, rows[k], done)
        w[p] = done
        if p < 15:
            turned = done[:, :128].T
            for g in range(p + 1, 16):
                rest = w[g]
                for k in range(8):
                    rest = rest - jnp.broadcast_to(turned[8 * g:8 * g + 8, k:k + 1], (8, 256)) * rows[k]
                w[g] = rest


def unit(rows):
    return jnp.where(
        lax.broadcasted_iota(jnp.int32, (rows, rows), 0) == lax.broadcasted_iota(jnp.int32, (rows, rows), 1), 1.0, 0.0)


def main_kernel(
    basis_in, momentum, gradient, ortho_out, right_out, sums_out,
    basis_all, loaded, buffer, partial, arrived, lefts, left, order, cross_part, slots, first, cross_all,
    gram_part, gram_send, gram_recv, gram_tiles, gram_all, work, block, sums,
    load_sems, basis_send, basis_recv, red_send, red_recv, cross_send, cross_recv, left_sems, sems,
):
    r, c = lax.axis_index("row"), lax.axis_index("col")
    core = lax.rem(c, 2)
    barrier, count = greet(r, c)
    loads = [
        pltpu.make_async_copy(basis_in, basis_all.at[r], load_sems.at[0]),
        pltpu.make_async_copy(momentum, loaded.at[0], load_sems.at[1]),
        pltpu.make_async_copy(gradient, loaded.at[1], load_sems.at[2]),
    ]
    for load in loads:
        load.start()
    work[:, 512:] = jnp.zeros((512, 512), F32)
    for b in range(4):
        work[128 * b:128 * b + 128, 512 + 128 * b:512 + 128 * b + 128] = unit(128)
    place = lax.broadcasted_iota(jnp.int32, (512, 512), 0)
    turn = (place >> 5) & 3
    far = 2 * (place >> 7) + 1 + (turn >> 1)
    source = jnp.where(place >= 480, r, jnp.where((turn & 1) == 0, r - far, r + far)) & (ROWS - 1)
    natural = source * 32 + (place & 31)
    order[...] = jnp.where(natural == lax.broadcasted_iota(jnp.int32, (512, 512), 1), 1.0, 0.0).astype(BF16)
    for load in loads:
        load.wait()
    buffer[...] = (loaded[0].astype(F32) + loaded[1].astype(F32)).astype(BF16)
    pl.semaphore_wait(barrier, count)

    gather = Gather(r, basis_all, basis_send, basis_recv)
    gather.start()

    def send_partial(w):
        if w < 3:
            for d in (2 * w + 1, 2 * w + 2):
                gather.forward(d)
            ids = [r - (2 * w + 1), r + (2 * w + 1), r - (2 * w + 2), r + (2 * w + 2)]
        else:
            gather.end(7)
            gather.end(8)
            ids = [r - 7, r + 7, r - 8, r]
        columns = jnp.concatenate([basis_all[ring(i)] for i in ids], axis=0)
        partial[w] = lax.dot_general(buffer[...], columns, NT, preferred_element_type=F32).astype(BF16)

        def rows_of(d):
            return partial.at[w, pl.ds(pl.multiple_of(d * 16, 16), 16), :]

        col_send(c, rows_of, arrived.at[w, c], left_sems.at[0, w], left_sems.at[1, w])
        arrived[w, c] = rows_of(c)[...]

    def send_left(w):
        wait_bytes(arrived.at[w, pl.ds(0, COLS - 1)], left_sems.at[1, w])
        total = arrived[w, 0].astype(F32)
        for k in range(1, COLS):
            total = total + arrived[w, k].astype(F32)
        lefts[w, c] = total.astype(BF16)
        col_send(c, lambda d: lefts.at[w, c], lefts.at[w, c], left_sems.at[2, w], left_sems.at[3, w])

    for w in range(4):
        send_partial(w)
        if w > 0:
            send_left(w - 1)
    send_left(3)
    for w in range(4):
        wait_bytes(arrived.at[w, pl.ds(0, COLS - 1)], left_sems.at[3, w])
    mixed = jnp.concatenate([lefts[w].reshape(512, 128) for w in range(4)], axis=1)
    left[...] = jnp.dot(mixed, order[...], preferred_element_type=F32).astype(BF16)

    quarter = c // 16
    for i in range(2):
        start = quarter if i == 0 else 3 - quarter
        lanes = left[:, pl.ds(pl.multiple_of(start * 128, 128), 128)]
        gram_part[i] = lax.dot_general(lanes, left[...], TN, preferred_element_type=F32)
    low = lax.rem(c, 16)
    for t in range(TILES):
        upper = t < 4 - quarter
        part = jnp.where(upper, 0, 1)
        row = jnp.where(upper, low, 15 - low)
        lane = jnp.where(upper, t + quarter, t - 1)
        gram_send[t] = gram_part[part, pl.ds(pl.multiple_of(row * 8, 8), 8), pl.ds(pl.multiple_of(lane * 128, 128), 128)]

    mine = lax.rem(r, 8)
    reducer = mine < TILES

    def send_tile(k, carry):
        d = ring(r + k)
        t = lax.rem(d, 8)

        @pl.when(t < TILES)
        def _():
            remote(gram_send.at[t], gram_recv.at[r], sems.at[0], sems.at[1], row=d).start()

        return carry

    lax.fori_loop(1, ROWS, send_tile, 0)

    for n in range(2):
        cross_part[256 * n:256 * n + 256, :] = lax.dot_general(
            left[:, 256 * n:256 * n + 256], buffer[...], TN, preferred_element_type=F32)
    reduce = Reduce(r, cross_part, slots, first, red_send, red_recv)
    reduce.start()

    @pl.when(reducer)
    def _():
        wait_bytes(gram_recv.at[pl.ds(0, ROWS - 1)], sems.at[1])
        gram_recv[r] = gram_send[mine]
        tile = gram_recv[0]
        for k in range(1, ROWS):
            tile = tile + gram_recv[k]
        gram_tiles[mine] = tile
        for k in (-3, -2, -1, 1, 2, 3, 4):
            remote(gram_tiles.at[mine], gram_tiles.at[mine], sems.at[2], sems.at[3], row=ring(r + k)).start()

    for k in range(2):
        reduce.forward(k)

    @pl.when(reducer)
    def _():
        wait_bytes(gram_recv.at[pl.ds(0, TILES - 1)], sems.at[3])

    @pl.when(jnp.logical_not(reducer))
    def _():
        wait_bytes(gram_recv.at[pl.ds(0, TILES)], sems.at[3])

    chip = c // 2
    gram_all[core, chip] = gram_tiles[...]

    def send_gram(k, carry):
        remote(gram_all.at[core, chip], gram_all.at[core, chip], sems.at[4], sems.at[5],
               col=lax.rem(c + 2 * k, COLS)).start()
        return carry

    lax.fori_loop(1, COLS // 2, send_gram, 0)
    for k in range(2, 4):
        reduce.forward(k)
    wait_bytes(gram_all.at[0, pl.ds(0, 15)], sems.at[5])
    sibling = remote(gram_all.at[core], gram_all.at[core], sems.at[6], sems.at[7], col=c + 1 - 2 * core)
    sibling.start()
    for k in range(4, 6):
        reduce.forward(k)
    sibling.wait_recv()

    def place_tiles(k, carry):
        kc = 2 * (k // 2) + lax.rem(k, 2)
        kq = kc // 16
        for t in range(TILES):
            upper = t < 4 - kq
            row = jnp.where(upper, kc, 63 - kc)
            lane = jnp.where(upper, t + kq, t - 1)
            work[pl.ds(pl.multiple_of(row * 8, 8), 8), pl.ds(pl.multiple_of(lane * 128, 128), 128)] = (
                gram_all[lax.rem(k, 2), k // 2, t])
        return carry

    lax.fori_loop(0, COLS, place_tiles, 0)
    cross_all[r] = reduce.end().astype(BF16)
    spread = Gather(r, cross_all, cross_send, cross_recv)
    spread.start()

    def factor_step(b, carry):
        rows = pl.ds(pl.multiple_of(128 * b, 128), 128)
        live = pl.ds(pl.multiple_of(128 * (b + 1), 128), 512)
        block[:, :, :128] = work[rows, rows].reshape(16, 8, 128)
        block[:, :, 128:] = unit(128).reshape(16, 8, 128)
        factor_block(block)
        inverse = block[:, :, 128:].reshape(128, 128)
        panel = lax.dot_general(inverse, work[rows, live], NN, precision=HIGHEST, preferred_element_type=F32)
        work[rows, live] = panel

        def trail(i, carry):
            lanes = pl.ds(pl.multiple_of(128 * i, 128), 128)
            work[lanes, live] = work[lanes, live] - lax.dot_general(
                work[rows, lanes], panel, TN, precision=HIGHEST, preferred_element_type=F32)
            return carry

        lax.fori_loop(b + 1, 4, trail, 0)

        @pl.when(b < 3)
        def _():
            spread.forward(2 * b + 1)
            spread.forward(2 * b + 2)

        return carry

    lax.fori_loop(0, 4, factor_step, 0)
    spread.end(7)
    spread.end(8)

    high, low_part = split(work[:, 512:])
    cross = cross_all[...].reshape(512, 896)
    right = jnp.dot(high, cross, preferred_element_type=F32) + jnp.dot(low_part, cross, preferred_element_type=F32)
    right_out[...] = right
    square_high, square_low = split(right * right)
    ones = jnp.ones((8, 896), BF16)
    total = (
        lax.dot_general(ones, square_high, NT, preferred_element_type=F32)
        + lax.dot_general(ones, square_low, NT, preferred_element_type=F32))
    sub = lax.broadcasted_iota(jnp.int32, (8, 128), 0)
    tile = total[:, :128]
    for q in range(1, 4):
        tile = jnp.where(sub == q, total[:, 128 * q:128 * q + 128], tile)
    sums[c] = tile
    col_send(c, lambda d: sums.at[c], sums.at[c], sems.at[8], sems.at[9])
    ortho_out[...] = (
        lax.dot_general(left[...], high, NT, preferred_element_type=F32)
        + lax.dot_general(left[...], low_part, NT, preferred_element_type=F32)).astype(BF16)

    gather.drain()
    reduce.drain()
    spread.drain()
    for w in range(4):
        wait_bytes(arrived.at[w, pl.ds(0, COLS - 1)], left_sems.at[0, w])
        wait_bytes(arrived.at[w, pl.ds(0, COLS - 1)], left_sems.at[2, w])

    @pl.when(reducer)
    def _():
        wait_bytes(gram_recv.at[pl.ds(0, 2 * TILES - 1)], sems.at[0])
        wait_bytes(gram_recv.at[pl.ds(0, 7)], sems.at[2])

    @pl.when(jnp.logical_not(reducer))
    def _():
        wait_bytes(gram_recv.at[pl.ds(0, 2 * TILES)], sems.at[0])

    wait_bytes(gram_all.at[0, pl.ds(0, 15)], sems.at[4])
    sibling.wait_send()
    wait_bytes(sums.at[pl.ds(0, COLS - 1)], sems.at[8])
    wait_bytes(sums.at[pl.ds(0, COLS - 1)], sems.at[9])
    total = sums[0]
    for k in range(1, COLS):
        total = total + sums[k]
    sums_out[...] = total


def main_call(basis_t, momentum, gradient):
    return pl.pallas_call(
        main_kernel,
        out_shape=[
            jax.ShapeDtypeStruct((512, 512), BF16),
            jax.ShapeDtypeStruct((512, 896), F32),
            jax.ShapeDtypeStruct((8, 128), F32),
        ],
        in_specs=[ANY] * 3,
        out_specs=[VMEM] * 3,
        scratch_shapes=[
            pltpu.VMEM((ROWS, 32, 896), BF16),
            pltpu.VMEM((2, 512, 896), BF16),
            pltpu.VMEM((512, 896), BF16),
            pltpu.VMEM((4, 512, 128), BF16),
            pltpu.VMEM((4, COLS, 16, 128), BF16),
            pltpu.VMEM((4, COLS, 16, 128), BF16),
            pltpu.VMEM((512, 512), BF16),
            pltpu.VMEM((512, 512), BF16),
            pltpu.VMEM((512, 896), F32),
            pltpu.VMEM((2, 9, 32, 896), BF16),
            pltpu.VMEM((2, 2, 32, 896), BF16),
            pltpu.VMEM((ROWS, 32, 896), BF16),
            pltpu.VMEM((2, 128, 512), F32),
            pltpu.VMEM((TILES, 8, 128), F32),
            pltpu.VMEM((ROWS, 8, 128), F32),
            pltpu.VMEM((TILES, 8, 128), F32),
            pltpu.VMEM((2, COLS // 2, TILES, 8, 128), F32),
            pltpu.VMEM((512, 1024), F32),
            pltpu.VMEM((16, 8, 256), F32),
            pltpu.VMEM((COLS, 8, 128), F32),
            DMA((3,)),
            DMA((2, 9)), DMA((2, 9)),
            DMA((2, 9)), DMA((2, 9)),
            DMA((2, 9)), DMA((2, 9)),
            DMA((4, 4)),
            DMA((10,)),
        ],
        compiler_params=pltpu.CompilerParams(
            collective_id=0, has_side_effects=True, vmem_limit_bytes=56 * 2**20),
    )(basis_t, momentum, gradient)


def out_kernel(ortho, right, sums, momentum, gradient, weight, new_weight, new_momentum, new_basis_t, values, basis, mine):
    @pl.when(pl.program_id(0) == 0)
    def _():
        scale = lax.rsqrt(sums[...] / FF + 1e-06).T
        for q in range(4):
            rows = slice(128 * q, 128 * q + 128)
            mine[rows, :] = right[rows, :] * scale[:, q:q + 1]
            values[rows, :] = right[rows, :].astype(BF16)
            basis[rows, :] = mine[rows, :].astype(BF16)
        r = lax.axis_index("row")
        new_basis_t[...] = mine[pl.ds(pl.multiple_of(r * 32, 32), 32), :].astype(BF16)

    correction = jnp.dot(ortho[...], values[...], preferred_element_type=F32)
    buffer = (momentum[...].astype(F32) + gradient[...].astype(F32)).astype(BF16).astype(F32)
    new_momentum[...] = (buffer - 0.2 * correction).astype(BF16)
    update = jnp.dot(ortho[...], basis[...], preferred_element_type=F32)
    new_weight[...] = (weight[...].astype(F32) - 0.5 * math.sqrt(D / RANK) * update).astype(BF16)


def out_call(ortho, right, sums, momentum, gradient, weight):
    slab = pl.BlockSpec((128, 896), lambda i: (i, 0))
    return pl.pallas_call(
        out_kernel,
        grid=(4,),
        out_shape=[
            jax.ShapeDtypeStruct((512, 896), BF16),
            jax.ShapeDtypeStruct((512, 896), BF16),
            jax.ShapeDtypeStruct((32, 896), BF16),
        ],
        in_specs=[
            pl.BlockSpec((128, 512), lambda i: (i, 0)),
            pl.BlockSpec((512, 896), lambda i: (0, 0)),
            pl.BlockSpec((8, 128), lambda i: (0, 0)),
            slab, slab, slab,
        ],
        out_specs=[slab, slab, pl.BlockSpec((32, 896), lambda i: (0, 0))],
        scratch_shapes=[
            pltpu.VMEM((512, 896), BF16),
            pltpu.VMEM((512, 896), BF16),
            pltpu.VMEM((512, 896), F32),
        ],
        compiler_params=pltpu.CompilerParams(vmem_limit_bytes=32 * 2**20),
    )(ortho, right, sums, momentum, gradient, weight)


def local(weight, gradient, momentum, basis):
    ortho, right, sums = main_call(basis.T, momentum, gradient)
    new_weight, new_momentum, new_basis_t = out_call(ortho, right, sums, momentum, gradient, weight)
    return new_weight, new_momentum, new_basis_t.T


def solution(mesh):
    return jax.shard_map(
        local,
        mesh=mesh,
        in_specs=(P("row", "col"), P("row", "col"), P("row", "col"), P("col", "row")),
        out_specs=(P("row", "col"), P("row", "col"), P("col", "row")),
        check_vma=False,
    )
```

time: 569 us -> 124 us (0.22); the launches traced: 559 us -> 124 us
  blocking collectives: 243 us -> 0 us
  waiting for transfers between devices: 136 us -> 0 us
  other arithmetic: 120 us -> 0 us
  Pallas kernels: 0 us -> 119 us
  matrix products: 30.6 us -> 0 us
  between operations: 17.4 us -> 0.68 us
  local copies, waits for them, and re-layouts: 12.9 us -> 4.4 us
    psum x2 -> x0, blocking collectives: 208 us -> none  [the longest x1 136 us: local(): left = lax.psum(partial_left, 'col').astype(jnp.bfloat16)]
    psum x1 -> x0, waiting for transfers between devices: 136 us -> none  [local(): cross = lax.psum(cross_part, 'row')]
    pallas_call x0 -> x2, Pallas kernels: none -> 119 us  [the longest x1 116 us: main_call(): pl.pallas_call(main_kernel, out_shape=[jax.ShapeDtypeStruct((512, 512), B...]
    another operation x17 -> x0, other arithmetic: 118 us -> none  [the longest x14 78.7 us: local(): factor = jnp.linalg.cholesky(gram)]
    all_gather x1 -> x0, blocking collectives: 34.9 us -> none  [local(): lax.all_gather(basis, 'row', axis=1, tiled=True)]
    another operation x20 -> x0, matrix products: 18.3 us -> none  [the longest x14 12.9 us: solve_right(): lax.linalg.triangular_solve(factor, values, left_side=False, lower=True,...]
    dot_general x5 -> x0, matrix products: 12.3 us -> none  [the longest x1 4.84 us: local(): lax.dot_general(ortho, right, (((1,), (1,)), ((), ())), precision=lax.Pre...]
    another operation x17 -> x0, local copies, waits for them, and re-layouts: 8.06 us -> none
  transfers between devices with their start and end apart: 1 -> 0, of which waited for: 1 -> 0; matrix products, arithmetic and copies ran while one was open for 0% -> 0% of each run, Pallas kernels for 0% -> 0%
where the time goes in v1:
time: 124 us
  Pallas kernels  119 us (96%)
  local copies, waits for them, and re-layouts  4.4 us (4%)
    pallas_call x1, Pallas kernels, main_call(): pl.pallas_call(main_kernel, out_shape=[jax.ShapeDtypeStruct((512, 512), B...  116 us
    unnamed x12, local copies, waits for them, and re-layouts  4.4 us
    pallas_call x1, Pallas kernels, out_call(): pl.pallas_call(out_kernel, grid=(4,), out_shape=[jax.ShapeDtypeStruct((51...  3.19 us

profile of v1, /device:TPU:1, one launch (start us, length us, event | category | flops | bytes accessed | tf_op | source)
XLA Modules:
  0.0 124.0 jit_solution(13796814595913483132)
XLA Ops:
  0.6 0.0 copy-start
  0.6 0.0 copy-start.1
  0.7 115.7 %shard_map.67 = (bf16[512,512]{1,0:T(8,128)(2,1)}, f32[512,896]{1,0:T(8,128)}, f32[8,128]{1,0:T(8,128)}) custom-call(bf16[32,896]{1,0:T(8,128)(2,1)} %bitcast.2, bf16[512,896]{1,0:T(8,128)(2,1)} %momentum.3, bf16[512,896]{1,0:T(8,128)(2,1)} %gradient.3), custom_call_target="tpu_custom_call" | custom-call | tf_op jit(solution)/shard_map/pallas_call | solution.py:444
  116.4 0.0 copy-done
  116.4 0.0 copy-done.1
  116.4 0.0 copy-start.2
  116.4 1.5 %copy-done.2 = f32[512,896]{1,0:T(8,128)S(1)} copy-done((f32[512,896]{1,0:T(8,128)S(1)}, f32[512,896]{1,0:T(8,128)}, u32[]{:S(2)}) %copy-start.2) | copy-done | bytes 1835032
  117.9 0.0 copy-start.3
  117.9 1.2 copy-done.3
  119.1 0.0 copy-start.4
  119.1 1.0 copy-done.4
  120.1 0.0 copy-start.5
  120.1 0.7 copy-done.5
  120.8 3.2 %shard_map.68 = (bf16[512,896]{1,0:T(8,128)(2,1)}, bf16[512,896]{1,0:T(8,128)(2,1)}, bf16[32,896]{1,0:T(8,128)(2,1)}) custom-call(bf16[512,512]{1,0:T(8,128)(2,1)S(1)} %copy-done.4, f32[512,896]{1,0:T(8,128)S(1)} %copy-done.2, f32[8,128]{1,0:T(8,128)S(1)} %copy-done.5, bf16[512,896]{1,0:T(8,128)(2,1)S(1)} %copy-done, bf16[512,896]{1,0:T(8,128)(2,1)S(1)} %copy-done.1, ...), custom_call_target="tpu_custom_call" | custom-call | tf_op jit(solution)/shard_map/pallas_call | solution.py:507
Async XLA Ops:
  0.6 115.8 %copy-start = (bf16[512,896]{1,0:T(8,128)(2,1)S(1)}, bf16[512,896]{1,0:T(8,128)(2,1)}, u32[]{:S(2)}) copy-start(bf16[512,896]{1,0:T(8,128)(2,1)} %momentum.3) | copy-start | bytes 2752516
  0.6 115.8 %copy-start.1 = (bf16[512,896]{1,0:T(8,128)(2,1)S(1)}, bf16[512,896]{1,0:T(8,128)(2,1)}, u32[]{:S(2)}) copy-start(bf16[512,896]{1,0:T(8,128)(2,1)} %gradient.3) | copy-start | bytes 2752516
  116.4 1.5 %copy-start.2 = (f32[512,896]{1,0:T(8,128)S(1)}, f32[512,896]{1,0:T(8,128)}, u32[]{:S(2)}) copy-start(f32[512,896]{1,0:T(8,128)} %get-tuple-element.10.right) | copy-start | bytes 5505028
  117.9 1.2 copy-start.3
  119.1 1.0 copy-start.4
  120.1 0.7 copy-start.5

commit v2 on v1

--- a/solution.py
+++ b/solution.py
@@ -13,9 +13,9 @@
 ROWS = 16
 COLS = 32
 TILES = 5
+LIMIT = 53 * 2**20
 F32 = jnp.float32
 BF16 = jnp.bfloat16
-HIGHEST = lax.Precision.HIGHEST
 MESH = pl.DeviceIdType.MESH
 VMEM = pl.BlockSpec(memory_space=pltpu.VMEM)
 ANY = pl.BlockSpec(memory_space=pl.ANY)
@@ -64,40 +64,43 @@
     def __init__(self, r, buf, send, recv):
         self.r, self.buf, self.send, self.recv = r, buf, send, recv
 
-    def message(self, way, d):
+    def message(self, way, d, h):
         sign = 1 if way == 0 else -1
         step = jnp.minimum(d, 2)
-        block = self.buf.at[ring(self.r - sign * (d - step))]
-        return remote(block, block, self.send.at[way, d], self.recv.at[way, d], row=ring(self.r + sign * step))
+        block = self.buf.at[ring(self.r - sign * (d - step)), pl.ds(16 * h, 16), :]
+        return remote(block, block, self.send.at[way, d, h], self.recv.at[way, d, h], row=ring(self.r + sign * step))
 
     def start(self):
-        for d in (2, 1):
+        for d in (1, 2):
+            for h in range(2):
+                for way in range(2):
+                    self.message(way, d, h).start()
+
+    def forward(self, d):
+        for h in range(2):
             for way in range(2):
-                self.message(way, d).start()
-
-    def forward(self, d):
-        for way in range(2):
-            self.message(way, d).wait_recv()
-            last = 8 - way
-
-            @pl.when(d + 2 <= last)
+                self.message(way, d, h).wait_recv()
+
+                @pl.when(d + 2 <= 8 - way)
+                def _():
+                    self.message(way, d + 2, h).start()
+
+    def end(self, d):
+        for h in range(2):
+            self.message(0, d, h).wait_recv()
+
+            @pl.when(d <= 7)
             def _():
-                self.message(way, d + 2).start()
-
-    def end(self, d):
-        self.message(0, d).wait_recv()
-
-        @pl.when(d <= 7)
-        def _():
-            self.message(1, d).wait_recv()
+                self.message(1, d, h).wait_recv()
 
     def drain(self):
         def one(d, carry):
-            self.message(0, d).wait_send()
-
-            @pl.when(d <= 7)
-            def _():
-                self.message(1, d).wait_send()
+            for h in range(2):
+                self.message(0, d, h).wait_send()
+
+                @pl.when(d <= 7)
+                def _():
+                    self.message(1, d, h).wait_send()
 
             return carry
 
@@ -109,52 +112,57 @@
         self.r, self.part, self.slots, self.first, self.send, self.recv = r, part, slots, first, send, recv
         self.size = RANK // ROWS
 
-    def own(self, block):
-        return self.part[pl.ds(pl.multiple_of(block * self.size, self.size), self.size), :]
-
-    def message(self, way, d, src):
+    def own(self, block, h):
+        return self.part[pl.ds(pl.multiple_of(block * self.size + 16 * h, 16), 16), :]
+
+    def message(self, way, d, h, src=None):
         sign = 1 if way == 0 else -1
+        slot = self.slots.at[way, d, pl.ds(16 * h, 16), :]
         return remote(
-            src, self.slots.at[way, d], self.send.at[way, d], self.recv.at[way, d],
+            slot if src is None else src, slot, self.send.at[way, d, h], self.recv.at[way, d, h],
             row=ring(self.r + sign * jnp.minimum(d, 2)))
 
     def start(self):
         for i in range(2):
+            for h in range(2):
+                for way in range(2):
+                    d = 8 - way - i
+                    here = self.first.at[way, i, pl.ds(16 * h, 16), :]
+                    here[...] = self.own(ring(self.r + (d if way == 0 else -d)), h).astype(BF16)
+                    self.message(way, d, h, here).start()
+
+    def forward(self, k):
+        for h in range(2):
             for way in range(2):
-                d = 8 - way - i
-                here = self.first.at[way, i]
-                here[...] = self.own(ring(self.r + (d if way == 0 else -d))).astype(BF16)
-                self.message(way, d, here).start()
-
-    def forward(self, k):
-        for way in range(2):
-            def go():
-                d = 6 - way - k
-                got = self.slots.at[way, d + 2]
-                self.message(way, d + 2, got).wait_recv()
-                got[...] = (got[...].astype(F32) + self.own(ring(self.r + (d if way == 0 else -d)))).astype(BF16)
-                self.message(way, d, got).start()
-
-            if way == 0:
-                go()
-            else:
-                pl.when(k < 5)(go)
-
-    def end(self):
-        total = self.own(self.r)
+                def go():
+                    d = 6 - way - k
+                    got = self.slots.at[way, d + 2, pl.ds(16 * h, 16), :]
+                    self.message(way, d + 2, h).wait_recv()
+                    term = self.own(ring(self.r + (d if way == 0 else -d)), h)
+                    got[...] = (got[...].astype(F32) + term).astype(BF16)
+                    self.message(way, d, h, got).start()
+
+                if way == 0:
+                    go()
+                else:
+                    pl.when(k < 5)(go)
+
+    def end(self, h):
+        total = self.own(self.r, h)
         for way in range(2):
             for d in (2, 1):
-                self.message(way, d, self.first.at[0, 0]).wait_recv()
-                total = total + self.slots[way, d].astype(F32)
+                self.message(way, d, h).wait_recv()
+                total = total + self.slots[way, d, pl.ds(16 * h, 16), :].astype(F32)
         return total
 
     def drain(self):
         def one(d, carry):
-            self.message(0, d, self.first.at[0, 0]).wait_send()
-
-            @pl.when(d <= 7)
-            def _():
-                self.message(1, d, self.first.at[0, 0]).wait_send()
+            for h in range(2):
+                self.message(0, d, h).wait_send()
+
+                @pl.when(d <= 7)
+                def _():
+                    self.message(1, d, h).wait_send()
 
             return carry
 
@@ -166,40 +174,85 @@
     return high, (x - high.astype(F32)).astype(BF16)
 
 
-def factor_block(w):
+def parts(x):
+    high = x.astype(BF16)
+    rest = x - high.astype(F32)
+    mid = rest.astype(BF16)
+    low = (rest - mid.astype(F32)).astype(BF16)
+    return (high, high, mid, high, low, mid), (high, mid, high, low, high, mid)
+
+
+def dot_exact(a, b):
+    return lax.dot_general(
+        jnp.concatenate(parts(a)[0], axis=0), jnp.concatenate(parts(b)[1], axis=0), TN, preferred_element_type=F32)
+
+
+def factor_block(w, spare):
     sub = lax.broadcasted_iota(jnp.int32, (8, 256), 0)
+    near = 3
 
     def twice(x):
         return jnp.concatenate([x, x], axis=1)
 
+    def column(x, k):
+        return jnp.broadcast_to(x[:, k:k + 1], (8, 128))
+
     for p in range(16):
         panel = w[p]
-        columns = [jnp.broadcast_to(panel[:, 8 * p + j:8 * p + j + 1], (8, 128)) for j in range(8)]
-        s = {}
+        rows = [jnp.broadcast_to(w[p, k:k + 1, :], (8, 256)) for k in range(8)]
+        s, u, root = {}, {}, {}
         for j in range(8):
+            spare[p % 2, j] = column(panel, 8 * p + j)
             for i in range(j + 1):
-                s[i, j] = jnp.broadcast_to(columns[j][i:i + 1, :], (8, 128))
-        rows = [jnp.broadcast_to(panel[k:k + 1, :], (8, 256)) for k in range(8)]
+                s[i, j] = jnp.broadcast_to(spare[p % 2, j, i:i + 1, :], (8, 128))
         for j in range(8):
-            root = lax.rsqrt(s[j, j])
-            u = {i: s[j, i] * root for i in range(j + 1, 8)}
+            root[j] = lax.rsqrt(s[j, j])
+            for i in range(j + 1, 8):
+                u[j, i] = s[j, i] * root[j]
             for i in range(j + 1, 8):
                 for l in range(i, 8):
-                    s[i, l] = s[i, l] - u[i] * u[l]
-            rows[j] = rows[j] * twice(root)
+                    s[i, l] = s[i, l] - u[j, i] * u[j, l]
+        for j in range(8):
+            rows[j] = rows[j] * twice(root[j])
             for i in range(j + 1, 8):
-                rows[i] = rows[i] - twice(u[i]) * rows[j]
+                rows[i] = rows[i] - twice(u[j, i]) * rows[j]
+        for g in range(p + 1, min(16, p + 1 + near)):
+            rest = w[g]
+            x = [column(rest, 8 * p + k) for k in range(8)]
+            for k in range(8):
+                x[k] = x[k] * root[k]
+                for l in range(k + 1, 8):
+                    x[l] = x[l] - x[k] * u[k, l]
+            taken = twice(x[0]) * rows[0]
+            for k in range(1, 8):
+                taken = taken + twice(x[k]) * rows[k]
+            w[g] = rest - taken
         done = rows[7]
         for k in range(7):
             done = jnp.where(sub == k, rows[k], done)
         w[p] = done
-        if p < 15:
-            turned = done[:, :128].T
-            for g in range(p + 1, 16):
-                rest = w[g]
-                for k in range(8):
-                    rest = rest - jnp.broadcast_to(turned[8 * g:8 * g + 8, k:k + 1], (8, 256)) * rows[k]
-                w[g] = rest
+        far = p + 1 + near
+        if far < 16:
+            taken = dot_exact(done[:, :128], done)
+            w[far:] = w[far:] - taken.reshape(16, 8, 256)[far:]
+
+
+def factor_rows(work, block, spare, b):
+    rows = pl.ds(pl.multiple_of(128 * b, 128), 128)
+    live = pl.ds(pl.multiple_of(128 * (b + 1), 128), 512)
+    block[:, :, :128] = work[rows, rows].reshape(16, 8, 128)
+    block[:, :, 128:] = unit(128).reshape(16, 8, 128)
+    factor_block(block, spare)
+    inverse = block[:, :, 128:].reshape(128, 128)
+    panel = lax.dot_general(
+        jnp.concatenate(parts(inverse)[0], axis=1), jnp.concatenate(parts(work[rows, live])[1], axis=0), NN,
+        preferred_element_type=F32)
+    work[rows, live] = panel
+
+    @pl.when(b < 3)
+    def _():
+        below = pl.ds(pl.multiple_of(128 * (b + 1), 128), 384)
+        work[below, live] = work[below, live] - dot_exact(panel[:, :384], panel)
 
 
 def unit(rows):
@@ -208,9 +261,9 @@
 
 
 def main_kernel(
-    basis_in, momentum, gradient, ortho_out, right_out, sums_out,
+    basis_in, momentum, gradient, weight, ortho_out, basis_out, momentum_out, weight_out,
     basis_all, loaded, buffer, partial, arrived, lefts, left, order, cross_part, slots, first, cross_all,
-    gram_part, gram_send, gram_recv, gram_tiles, gram_all, work, block, sums,
+    gram_part, gram_send, gram_recv, gram_tiles, gram_all, work, block, spare, sums,
     load_sems, basis_send, basis_recv, red_send, red_recv, cross_send, cross_recv, left_sems, sems,
 ):
     r, c = lax.axis_index("row"), lax.axis_index("col")
@@ -223,7 +276,9 @@
     ]
     for load in loads:
         load.start()
-    work[:, 512:] = jnp.zeros((512, 512), F32)
+    keep = pltpu.make_async_copy(weight, weight_out, load_sems.at[3])
+    keep.start()
+    work[...] = jnp.zeros((896, 1024), F32)
     for b in range(4):
         work[128 * b:128 * b + 128, 512 + 128 * b:512 + 128 * b + 128] = unit(128)
     place = lax.broadcasted_iota(jnp.int32, (512, 512), 0)
@@ -362,27 +417,13 @@
         return carry
 
     lax.fori_loop(0, COLS, place_tiles, 0)
-    cross_all[r] = reduce.end().astype(BF16)
+    for h in range(2):
+        cross_all[r, pl.ds(16 * h, 16), :] = reduce.end(h).astype(BF16)
     spread = Gather(r, cross_all, cross_send, cross_recv)
     spread.start()
 
     def factor_step(b, carry):
-        rows = pl.ds(pl.multiple_of(128 * b, 128), 128)
-        live = pl.ds(pl.multiple_of(128 * (b + 1), 128), 512)
-        block[:, :, :128] = work[rows, rows].reshape(16, 8, 128)
-        block[:, :, 128:] = unit(128).reshape(16, 8, 128)
-        factor_block(block)
-        inverse = block[:, :, 128:].reshape(128, 128)
-        panel = lax.dot_general(inverse, work[rows, live], NN, precision=HIGHEST, preferred_element_type=F32)
-        work[rows, live] = panel
-
-        def trail(i, carry):
-            lanes = pl.ds(pl.multiple_of(128 * i, 128), 128)
-            work[lanes, live] = work[lanes, live] - lax.dot_general(
-                work[rows, lanes], panel, TN, precision=HIGHEST, preferred_element_type=F32)
-            return carry
-
-        lax.fori_loop(b + 1, 4, trail, 0)
+        factor_rows(work, block, spare, b)
 
         @pl.when(b < 3)
         def _():
@@ -395,10 +436,9 @@
     spread.end(7)
     spread.end(8)
 
-    high, low_part = split(work[:, 512:])
+    high, low_part = split(work[:512, 512:])
     cross = cross_all[...].reshape(512, 896)
     right = jnp.dot(high, cross, preferred_element_type=F32) + jnp.dot(low_part, cross, preferred_element_type=F32)
-    right_out[...] = right
     square_high, square_low = split(right * right)
     ones = jnp.ones((8, 896), BF16)
     total = (
@@ -410,9 +450,13 @@
         tile = jnp.where(sub == q, total[:, 128 * q:128 * q + 128], tile)
     sums[c] = tile
     col_send(c, lambda d: sums.at[c], sums.at[c], sems.at[8], sems.at[9])
-    ortho_out[...] = (
+    ortho = (
         lax.dot_general(left[...], high, NT, preferred_element_type=F32)
         + lax.dot_general(left[...], low_part, NT, preferred_element_type=F32)).astype(BF16)
+    ortho_out[...] = ortho
+    correction = jnp.dot(ortho, right.astype(BF16), preferred_element_type=F32)
+    momentum_out[...] = (buffer[...].astype(F32) - 0.2 * correction).astype(BF16)
+    keep.wait()
 
     gather.drain()
     reduce.drain()
@@ -437,19 +481,22 @@
     total = sums[0]
     for k in range(1, COLS):
         total = total + sums[k]
-    sums_out[...] = total
-
-
-def main_call(basis_t, momentum, gradient):
+    scale = lax.rsqrt(total / FF + 1e-06).T
+    for q in range(4):
+        basis_out[128 * q:128 * q + 128, :] = (right[128 * q:128 * q + 128, :] * scale[:, q:q + 1]).astype(BF16)
+
+
+def main_call(basis_t, momentum, gradient, weight):
     return pl.pallas_call(
         main_kernel,
         out_shape=[
             jax.ShapeDtypeStruct((512, 512), BF16),
-            jax.ShapeDtypeStruct((512, 896), F32),
-            jax.ShapeDtypeStruct((8, 128), F32),
+            jax.ShapeDtypeStruct((512, 896), BF16),
+            jax.ShapeDtypeStruct((512, 896), BF16),
+            jax.ShapeDtypeStruct((512, 896), BF16),
         ],
-        in_specs=[ANY] * 3,
-        out_specs=[VMEM] * 3,
+        in_specs=[ANY] * 4,
+        out_specs=[VMEM] * 4,
         scratch_shapes=[
             pltpu.VMEM((ROWS, 32, 896), BF16),
             pltpu.VMEM((2, 512, 896), BF16),
@@ -468,70 +515,58 @@
             pltpu.VMEM((ROWS, 8, 128), F32),
             pltpu.VMEM((TILES, 8, 128), F32),
             pltpu.VMEM((2, COLS // 2, TILES, 8, 128), F32),
-            pltpu.VMEM((512, 1024), F32),
+            pltpu.VMEM((896, 1024), F32),
             pltpu.VMEM((16, 8, 256), F32),
+            pltpu.VMEM((2, 8, 8, 128), F32),
             pltpu.VMEM((COLS, 8, 128), F32),
-            DMA((3,)),
-            DMA((2, 9)), DMA((2, 9)),
-            DMA((2, 9)), DMA((2, 9)),
-            DMA((2, 9)), DMA((2, 9)),
+            DMA((4,)),
+            DMA((2, 9, 2)), DMA((2, 9, 2)),
+            DMA((2, 9, 2)), DMA((2, 9, 2)),
+            DMA((2, 9, 2)), DMA((2, 9, 2)),
             DMA((4, 4)),
             DMA((10,)),
         ],
         compiler_params=pltpu.CompilerParams(
-            collective_id=0, has_side_effects=True, vmem_limit_bytes=56 * 2**20),
-    )(basis_t, momentum, gradient)
-
-
-def out_kernel(ortho, right, sums, momentum, gradient, weight, new_weight, new_momentum, new_basis_t, values, basis, mine):
-    @pl.when(pl.program_id(0) == 0)
-    def _():
-        scale = lax.rsqrt(sums[...] / FF + 1e-06).T
-        for q in range(4):
-            rows = slice(128 * q, 128 * q + 128)
-            mine[rows, :] = right[rows, :] * scale[:, q:q + 1]
-            values[rows, :] = right[rows, :].astype(BF16)
-            basis[rows, :] = mine[rows, :].astype(BF16)
-        r = lax.axis_index("row")
-        new_basis_t[...] = mine[pl.ds(pl.multiple_of(r * 32, 32), 32), :].astype(BF16)
-
-    correction = jnp.dot(ortho[...], values[...], preferred_element_type=F32)
-    buffer = (momentum[...].astype(F32) + gradient[...].astype(F32)).astype(BF16).astype(F32)
-    new_momentum[...] = (buffer - 0.2 * correction).astype(BF16)
-    update = jnp.dot(ortho[...], basis[...], preferred_element_type=F32)
-    new_weight[...] = (weight[...].astype(F32) - 0.5 * math.sqrt(D / RANK) * update).astype(BF16)
-
-
-def out_call(ortho, right, sums, momentum, gradient, weight):
-    slab = pl.BlockSpec((128, 896), lambda i: (i, 0))
+            collective_id=0, has_side_effects=True, vmem_limit_bytes=LIMIT),
+    )(basis_t, momentum, gradient, weight)
+
+
+def out_kernel(ortho, basis, momentum, weight, new_weight, new_momentum, new_basis_t, done, sems):
+    r = lax.axis_index("row")
+    copies = [
+        pltpu.make_async_copy(momentum, new_momentum, sems.at[0]),
+        pltpu.make_async_copy(basis.at[pl.ds(pl.multiple_of(r * 32, 32), 32), :], new_basis_t, sems.at[1]),
+    ]
+    for copy in copies:
+        copy.start()
+    for q in range(4):
+        rows = pl.ds(128 * q, 128)
+        update = jnp.dot(ortho[rows, :], basis[...], preferred_element_type=F32)
+        done[rows, :] = (weight[rows, :].astype(F32) - 0.5 * math.sqrt(D / RANK) * update).astype(BF16)
+        copies.append(pltpu.make_async_copy(done.at[rows, :], new_weight.at[rows, :], sems.at[2 + q]))
+        copies[2 + q].start()
+    for copy in copies:
+        copy.wait()
+
+
+def out_call(ortho, basis, momentum, weight):
     return pl.pallas_call(
         out_kernel,
-        grid=(4,),
         out_shape=[
             jax.ShapeDtypeStruct((512, 896), BF16),
             jax.ShapeDtypeStruct((512, 896), BF16),
             jax.ShapeDtypeStruct((32, 896), BF16),
         ],
-        in_specs=[
-            pl.BlockSpec((128, 512), lambda i: (i, 0)),
-            pl.BlockSpec((512, 896), lambda i: (0, 0)),
-            pl.BlockSpec((8, 128), lambda i: (0, 0)),
-            slab, slab, slab,
-        ],
-        out_specs=[slab, slab, pl.BlockSpec((32, 896), lambda i: (0, 0))],
-        scratch_shapes=[
-            pltpu.VMEM((512, 896), BF16),
-            pltpu.VMEM((512, 896), BF16),
-            pltpu.VMEM((512, 896), F32),
-        ],
-        compiler_params=pltpu.CompilerParams(vmem_limit_bytes=32 * 2**20),
-    )(ortho, right, sums, momentum, gradient, weight)
+        in_specs=[VMEM] * 4,
+        out_specs=[ANY] * 3,
+        scratch_shapes=[pltpu.VMEM((512, 896), BF16), DMA((6,))],
+        compiler_params=pltpu.CompilerParams(vmem_limit_bytes=LIMIT),
+    )(ortho, basis, momentum, weight)
 
 
 def local(weight, gradient, momentum, basis):
-    ortho, right, sums = main_call(basis.T, momentum, gradient)
-    new_weight, new_momentum, new_basis_t = out_call(ortho, right, sums, momentum, gradient, weight)
-    return new_weight, new_momentum, new_basis_t.T
+    outputs = out_call(*main_call(basis.T, momentum, gradient, weight))
+    return outputs[0], outputs[1], outputs[2].T
 
 
 def solution(mesh):

time: 124 us -> 112 us (0.903)
  Pallas kernels: 119 us -> 110 us
  local copies, waits for them, and re-layouts: 4.4 us -> 0.81 us
    pallas_call x1, Pallas kernels: 116 us -> 107 us  [main_call(): pl.pallas_call(main_kernel, out_shape=[jax.ShapeDtypeStruct((512, 512), B...]
    unnamed x12 -> x2, local copies, waits for them, and re-layouts: 4.4 us -> 0.81 us
where the time goes in v2:
time: 112 us; the launch traced here: 111 us
  Pallas kernels  110 us (98%)
    pallas_call x1, Pallas kernels, main_call(): pl.pallas_call(main_kernel, out_shape=[jax.ShapeDtypeStruct((512, 512), B...  107 us
    pallas_call x1, Pallas kernels, out_call(): pl.pallas_call(out_kernel, out_shape=[jax.ShapeDtypeStruct((512, 896), BF...  3.2 us

profile of v2, /device:TPU:1, one launch (start us, length us, event | category | flops | bytes accessed | tf_op | source)
XLA Modules:
  0.0 111.3 jit_solution(16741363264546765350)
XLA Ops:
  0.6 0.0 copy-start
  0.6 0.8 copy-done
  1.5 106.7 %shard_map.67 = (bf16[512,512]{1,0:T(8,128)(2,1)S(1)}, bf16[512,896]{1,0:T(8,128)(2,1)}, bf16[512,896]{1,0:T(8,128)(2,1)}, bf16[512,896]{1,0:T(8,128)(2,1)}) custom-call(bf16[32,896]{1,0:T(8,128)(2,1)S(1)} %bitcast.2, bf16[512,896]{1,0:T(8,128)(2,1)} %momentum.1, bf16[512,896]{1,0:T(8,128)(2,1)} %gradient.1, bf16[512,896]{1,0:T(8,128)(2,1)} %weight.1), custom_call_target="tpu_custom_call" | custom-call | tf_op jit(solution)/shard_map/pallas_call | solution.py:490
  108.1 3.2 %shard_map.68 = (bf16[512,896]{1,0:T(8,128)(2,1)}, bf16[512,896]{1,0:T(8,128)(2,1)}, bf16[32,896]{1,0:T(8,128)(2,1)}) custom-call(bf16[512,512]{1,0:T(8,128)(2,1)S(1)} %get-tuple-element.10.ortho, bf16[512,896]{1,0:T(8,128)(2,1)} %get-tuple-element.11.basis, bf16[512,896]{1,0:T(8,128)(2,1)} %get-tuple-element.12.momentum, ...), custom_call_target="tpu_custom_call" | custom-call | tf_op jit(solution)/shard_map/pallas_call | solution.py:553
Async XLA Ops:
  0.6 0.8 copy-start

commit v3 on v2

--- a/solution.py
+++ b/solution.py
@@ -53,11 +53,11 @@
 
 def col_send(c, src_of, dst, send, recv):
     def one(k, carry):
-        d = lax.rem(c + k, COLS)
+        d = lax.rem(c + 1 + lax.rem(k + COLS // 2 - 1, COLS - 1), COLS)
         remote(src_of(d), dst, send, recv, col=d).start()
         return carry
 
-    lax.fori_loop(1, COLS, one, 0)
+    lax.fori_loop(0, COLS - 1, one, 0)
 
 
 class Gather:
@@ -66,12 +66,12 @@
 
     def message(self, way, d, h):
         sign = 1 if way == 0 else -1
-        step = jnp.minimum(d, 2)
+        step = 2 - d % 2
         block = self.buf.at[ring(self.r - sign * (d - step)), pl.ds(16 * h, 16), :]
         return remote(block, block, self.send.at[way, d, h], self.recv.at[way, d, h], row=ring(self.r + sign * step))
 
     def start(self):
-        for d in (1, 2):
+        for d in (2, 1):
             for h in range(2):
                 for way in range(2):
                     self.message(way, d, h).start()
@@ -80,31 +80,22 @@
         for h in range(2):
             for way in range(2):
                 self.message(way, d, h).wait_recv()
-
-                @pl.when(d + 2 <= 8 - way)
-                def _():
+                if d + 2 <= 8 - way:
                     self.message(way, d + 2, h).start()
+                self.message(way, d + 1, h).start()
 
     def end(self, d):
         for h in range(2):
-            self.message(0, d, h).wait_recv()
-
-            @pl.when(d <= 7)
-            def _():
-                self.message(1, d, h).wait_recv()
+            for way in range(2):
+                if d <= 8 - way:
+                    self.message(way, d, h).wait_recv()
 
     def drain(self):
-        def one(d, carry):
+        for d in range(1, 9):
             for h in range(2):
-                self.message(0, d, h).wait_send()
-
-                @pl.when(d <= 7)
-                def _():
-                    self.message(1, d, h).wait_send()
-
-            return carry
-
-        lax.fori_loop(1, 9, one, 0)
+                for way in range(2):
+                    if d <= 8 - way:
+                        self.message(way, d, h).wait_send()
 
 
 class Reduce:
@@ -112,61 +103,58 @@
         self.r, self.part, self.slots, self.first, self.send, self.recv = r, part, slots, first, send, recv
         self.size = RANK // ROWS
 
-    def own(self, block, h):
+    def own(self, way, d, h):
+        block = ring(self.r + (d if way == 0 else -d))
         return self.part[pl.ds(pl.multiple_of(block * self.size + 16 * h, 16), 16), :]
+
+    def slot(self, way, d, h):
+        return self.slots.at[way, d, pl.ds(16 * h, 16), :]
 
     def message(self, way, d, h, src=None):
         sign = 1 if way == 0 else -1
-        slot = self.slots.at[way, d, pl.ds(16 * h, 16), :]
+        slot = self.slot(way, d, h)
         return remote(
             slot if src is None else src, slot, self.send.at[way, d, h], self.recv.at[way, d, h],
-            row=ring(self.r + sign * jnp.minimum(d, 2)))
+            row=ring(self.r + sign * (2 - d % 2)))
+
+    def give(self, way, d, h):
+        here = self.first.at[way, d // 2, pl.ds(16 * h, 16), :]
+        here[...] = self.own(way, d, h).astype(BF16)
+        self.message(way, d, h, here).start()
 
     def start(self):
-        for i in range(2):
+        for h in range(2):
+            self.give(0, 8, h)
+            self.give(1, 7, h)
+            self.give(0, 7, h)
+
+    def forward(self, d):
+        for h in range(2):
+            for way in range(2):
+                total = self.own(way, d, h)
+                for far in (d + 1, d + 2):
+                    if far <= 8 - way:
+                        self.message(way, far, h).wait_recv()
+                        total = total + self.slot(way, far, h)[...].astype(F32)
+                here = self.slot(way, d + 1, h)
+                here[...] = total.astype(BF16)
+                self.message(way, d, h, here).start()
+                self.give(way, d - 1, h)
+
+    def end(self, h):
+        total = self.own(0, 0, h)
+        for way in range(2):
+            for d in (1, 2):
+                self.message(way, d, h).wait_recv()
+                total = total + self.slot(way, d, h)[...].astype(F32)
+        return total
+
+    def drain(self):
+        for d in range(1, 9):
             for h in range(2):
                 for way in range(2):
-                    d = 8 - way - i
-                    here = self.first.at[way, i, pl.ds(16 * h, 16), :]
-                    here[...] = self.own(ring(self.r + (d if way == 0 else -d)), h).astype(BF16)
-                    self.message(way, d, h, here).start()
-
-    def forward(self, k):
-        for h in range(2):
-            for way in range(2):
-                def go():
-                    d = 6 - way - k
-                    got = self.slots.at[way, d + 2, pl.ds(16 * h, 16), :]
-                    self.message(way, d + 2, h).wait_recv()
-                    term = self.own(ring(self.r + (d if way == 0 else -d)), h)
-                    got[...] = (got[...].astype(F32) + term).astype(BF16)
-                    self.message(way, d, h, got).start()
-
-                if way == 0:
-                    go()
-                else:
-                    pl.when(k < 5)(go)
-
-    def end(self, h):
-        total = self.own(self.r, h)
-        for way in range(2):
-            for d in (2, 1):
-                self.message(way, d, h).wait_recv()
-                total = total + self.slots[way, d, pl.ds(16 * h, 16), :].astype(F32)
-        return total
-
-    def drain(self):
-        def one(d, carry):
-            for h in range(2):
-                self.message(0, d, h).wait_send()
-
-                @pl.when(d <= 7)
-                def _():
-                    self.message(1, d, h).wait_send()
-
-            return carry
-
-        lax.fori_loop(1, 9, one, 0)
+                    if d <= 8 - way:
+                        self.message(way, d, h).wait_send()
 
 
 def split(x):
@@ -187,7 +175,7 @@
         jnp.concatenate(parts(a)[0], axis=0), jnp.concatenate(parts(b)[1], axis=0), TN, preferred_element_type=F32)
 
 
-def factor_block(w, spare):
+def factor_block(w, spare, midway):
     sub = lax.broadcasted_iota(jnp.int32, (8, 256), 0)
     near = 3
 
@@ -198,6 +186,8 @@
         return jnp.broadcast_to(x[:, k:k + 1], (8, 128))
 
     for p in range(16):
+        if p == 8:
+            midway()
         panel = w[p]
         rows = [jnp.broadcast_to(w[p, k:k + 1, :], (8, 256)) for k in range(8)]
         s, u, root = {}, {}, {}
@@ -237,12 +227,12 @@
             w[far:] = w[far:] - taken.reshape(16, 8, 256)[far:]
 
 
-def factor_rows(work, block, spare, b):
+def factor_rows(work, block, spare, b, midway):
     rows = pl.ds(pl.multiple_of(128 * b, 128), 128)
     live = pl.ds(pl.multiple_of(128 * (b + 1), 128), 512)
     block[:, :, :128] = work[rows, rows].reshape(16, 8, 128)
     block[:, :, 128:] = unit(128).reshape(16, 8, 128)
-    factor_block(block, spare)
+    factor_block(block, spare, midway)
     inverse = block[:, :, 128:].reshape(128, 128)
     panel = lax.dot_general(
         jnp.concatenate(parts(inverse)[0], axis=1), jnp.concatenate(parts(work[rows, live])[1], axis=0), NN,
@@ -297,8 +287,8 @@
 
     def send_partial(w):
         if w < 3:
-            for d in (2 * w + 1, 2 * w + 2):
-                gather.forward(d)
+            gather.forward(2 * w + 2)
+            gather.end(2 * w + 1)
             ids = [r - (2 * w + 1), r + (2 * w + 1), r - (2 * w + 2), r + (2 * w + 2)]
         else:
             gather.end(7)
@@ -364,6 +354,7 @@
             left[:, 256 * n:256 * n + 256], buffer[...], TN, preferred_element_type=F32)
     reduce = Reduce(r, cross_part, slots, first, red_send, red_recv)
     reduce.start()
+    reduce.forward(6)
 
     @pl.when(reducer)
     def _():
@@ -376,8 +367,7 @@
         for k in (-3, -2, -1, 1, 2, 3, 4):
             remote(gram_tiles.at[mine], gram_tiles.at[mine], sems.at[2], sems.at[3], row=ring(r + k)).start()
 
-    for k in range(2):
-        reduce.forward(k)
+    reduce.forward(4)
 
     @pl.when(reducer)
     def _():
@@ -396,13 +386,10 @@
         return carry
 
     lax.fori_loop(1, COLS // 2, send_gram, 0)
-    for k in range(2, 4):
-        reduce.forward(k)
+    reduce.forward(2)
     wait_bytes(gram_all.at[0, pl.ds(0, 15)], sems.at[5])
     sibling = remote(gram_all.at[core], gram_all.at[core], sems.at[6], sems.at[7], col=c + 1 - 2 * core)
     sibling.start()
-    for k in range(4, 6):
-        reduce.forward(k)
     sibling.wait_recv()
 
     def place_tiles(k, carry):
@@ -417,24 +404,32 @@
         return carry
 
     lax.fori_loop(0, COLS, place_tiles, 0)
-    for h in range(2):
-        cross_all[r, pl.ds(16 * h, 16), :] = reduce.end(h).astype(BF16)
     spread = Gather(r, cross_all, cross_send, cross_recv)
-    spread.start()
 
     def factor_step(b, carry):
-        factor_rows(work, block, spare, b)
-
-        @pl.when(b < 3)
+        def midway():
+            @pl.when(b == 0)
+            def _():
+                for h in range(2):
+                    cross_all[r, pl.ds(16 * h, 16), :] = reduce.end(h).astype(BF16)
+                spread.start()
+
+            @pl.when(b == 1)
+            def _():
+                spread.forward(2)
+
+        factor_rows(work, block, spare, b, midway)
+
+        @pl.when(b == 2)
         def _():
-            spread.forward(2 * b + 1)
-            spread.forward(2 * b + 2)
+            spread.forward(4)
 
         return carry
 
     lax.fori_loop(0, 4, factor_step, 0)
-    spread.end(7)
-    spread.end(8)
+    spread.forward(6)
+    for d in (1, 3, 5, 7, 8):
+        spread.end(d)
 
     high, low_part = split(work[:512, 512:])
     cross = cross_all[...].reshape(512, 896)
@@ -508,7 +503,7 @@
             pltpu.VMEM((512, 512), BF16),
             pltpu.VMEM((512, 896), F32),
             pltpu.VMEM((2, 9, 32, 896), BF16),
-            pltpu.VMEM((2, 2, 32, 896), BF16),
+            pltpu.VMEM((2, 5, 32, 896), BF16),
             pltpu.VMEM((ROWS, 32, 896), BF16),
             pltpu.VMEM((2, 128, 512), F32),
             pltpu.VMEM((TILES, 8, 128), F32),

time: 112 us -> 107 us (0.955)
  Pallas kernels: 110 us -> 105 us
    pallas_call x1, Pallas kernels: 107 us -> 102 us  [main_call(): pl.pallas_call(main_kernel, out_shape=[jax.ShapeDtypeStruct((512, 512), B...]
where the time goes in v3:
time: 107 us; the launch traced here: 106 us
  Pallas kernels  105 us (98%)
    pallas_call x1, Pallas kernels, main_call(): pl.pallas_call(main_kernel, out_shape=[jax.ShapeDtypeStruct((512, 512), B...  102 us
    pallas_call x1, Pallas kernels, out_call(): pl.pallas_call(out_kernel, out_shape=[jax.ShapeDtypeStruct((512, 896), BF...  3.2 us

profile of v3, /device:TPU:1, one launch (start us, length us, event | category | flops | bytes accessed | tf_op | source)
XLA Modules:
  0.0 106.4 jit_solution(8264886737785893361)
XLA Ops:
  0.6 0.0 copy-start
  0.6 0.8 copy-done
  1.5 101.7 %shard_map.67 = (bf16[512,512]{1,0:T(8,128)(2,1)S(1)}, bf16[512,896]{1,0:T(8,128)(2,1)}, bf16[512,896]{1,0:T(8,128)(2,1)}, bf16[512,896]{1,0:T(8,128)(2,1)}) custom-call(bf16[32,896]{1,0:T(8,128)(2,1)S(1)} %bitcast.2, bf16[512,896]{1,0:T(8,128)(2,1)} %momentum.1, bf16[512,896]{1,0:T(8,128)(2,1)} %gradient.1, bf16[512,896]{1,0:T(8,128)(2,1)} %weight.1), custom_call_target="tpu_custom_call" | custom-call | tf_op jit(solution)/shard_map/pallas_call | solution.py:485
  103.2 3.2 %shard_map.68 = (bf16[512,896]{1,0:T(8,128)(2,1)}, bf16[512,896]{1,0:T(8,128)(2,1)}, bf16[32,896]{1,0:T(8,128)(2,1)}) custom-call(bf16[512,512]{1,0:T(8,128)(2,1)S(1)} %get-tuple-element.10.ortho, bf16[512,896]{1,0:T(8,128)(2,1)} %get-tuple-element.11.basis, bf16[512,896]{1,0:T(8,128)(2,1)} %get-tuple-element.12.momentum, ...), custom_call_target="tpu_custom_call" | custom-call | tf_op jit(solution)/shard_map/pallas_call | solution.py:548
Async XLA Ops:
  0.6 0.8 copy-start

commit v4 on v3

--- a/solution.py
+++ b/solution.py
@@ -271,11 +271,10 @@
     work[...] = jnp.zeros((896, 1024), F32)
     for b in range(4):
         work[128 * b:128 * b + 128, 512 + 128 * b:512 + 128 * b + 128] = unit(128)
-    place = lax.broadcasted_iota(jnp.int32, (512, 512), 0)
-    turn = (place >> 5) & 3
-    far = 2 * (place >> 7) + 1 + (turn >> 1)
-    source = jnp.where(place >= 480, r, jnp.where((turn & 1) == 0, r - far, r + far)) & (ROWS - 1)
-    natural = source * 32 + (place & 31)
+    position = lax.broadcasted_iota(jnp.int32, (512, 512), 0)
+    turn = position >> 5
+    far = (turn + 1) >> 1
+    natural = (jnp.where((turn & 1) == 1, r - far, r + far) & (ROWS - 1)) * 32 + (position & 31)
     order[...] = jnp.where(natural == lax.broadcasted_iota(jnp.int32, (512, 512), 1), 1.0, 0.0).astype(BF16)
     for load in loads:
         load.wait()
@@ -285,16 +284,17 @@
     gather = Gather(r, basis_all, basis_send, basis_recv)
     gather.start()
 
+    def blocks(w):
+        return [ring(r - (m + 1) // 2 if m % 2 else r + m // 2) for m in range(4 * w, 4 * w + 4)]
+
     def send_partial(w):
         if w < 3:
             gather.forward(2 * w + 2)
             gather.end(2 * w + 1)
-            ids = [r - (2 * w + 1), r + (2 * w + 1), r - (2 * w + 2), r + (2 * w + 2)]
         else:
             gather.end(7)
             gather.end(8)
-            ids = [r - 7, r + 7, r - 8, r]
-        columns = jnp.concatenate([basis_all[ring(i)] for i in ids], axis=0)
+        columns = jnp.concatenate([basis_all[i] for i in blocks(w)], axis=0)
         partial[w] = lax.dot_general(buffer[...], columns, NT, preferred_element_type=F32).astype(BF16)
 
         def rows_of(d):
@@ -311,13 +311,29 @@
         lefts[w, c] = total.astype(BF16)
         col_send(c, lambda d: lefts.at[w, c], lefts.at[w, c], left_sems.at[2, w], left_sems.at[3, w])
 
-    for w in range(4):
-        send_partial(w)
-        if w > 0:
-            send_left(w - 1)
+    reduce = Reduce(r, cross_part, slots, first, red_send, red_recv)
+
+    def add_cross(w):
+        wait_bytes(arrived.at[w, pl.ds(0, COLS - 1)], left_sems.at[3, w])
+        part = lax.dot_general(lefts[w].reshape(512, 128), buffer[...], TN, preferred_element_type=F32)
+        for i, b in enumerate(blocks(w)):
+            cross_part[pl.ds(pl.multiple_of(32 * ring(b + 8), 32), 32), :] = part[32 * i:32 * i + 32, :]
+
+    send_partial(0)
+    send_partial(1)
+    send_left(0)
+    send_partial(2)
+    send_left(1)
+    add_cross(0)
+    reduce.start()
+    send_partial(3)
+    send_left(2)
+    add_cross(1)
+    reduce.forward(6)
     send_left(3)
-    for w in range(4):
-        wait_bytes(arrived.at[w, pl.ds(0, COLS - 1)], left_sems.at[3, w])
+    add_cross(2)
+    reduce.forward(4)
+    add_cross(3)
     mixed = jnp.concatenate([lefts[w].reshape(512, 128) for w in range(4)], axis=1)
     left[...] = jnp.dot(mixed, order[...], preferred_element_type=F32).astype(BF16)
 
@@ -349,12 +365,7 @@
 
     lax.fori_loop(1, ROWS, send_tile, 0)
 
-    for n in range(2):
-        cross_part[256 * n:256 * n + 256, :] = lax.dot_general(
-            left[:, 256 * n:256 * n + 256], buffer[...], TN, preferred_element_type=F32)
-    reduce = Reduce(r, cross_part, slots, first, red_send, red_recv)
-    reduce.start()
-    reduce.forward(6)
+    reduce.forward(2)
 
     @pl.when(reducer)
     def _():
@@ -367,7 +378,10 @@
         for k in (-3, -2, -1, 1, 2, 3, 4):
             remote(gram_tiles.at[mine], gram_tiles.at[mine], sems.at[2], sems.at[3], row=ring(r + k)).start()
 
-    reduce.forward(4)
+    for h in range(2):
+        cross_all[r, pl.ds(16 * h, 16), :] = reduce.end(h).astype(BF16)
+    spread = Gather(r, cross_all, cross_send, cross_recv)
+    spread.start()
 
     @pl.when(reducer)
     def _():
@@ -386,10 +400,11 @@
         return carry
 
     lax.fori_loop(1, COLS // 2, send_gram, 0)
-    reduce.forward(2)
+    spread.forward(2)
     wait_bytes(gram_all.at[0, pl.ds(0, 15)], sems.at[5])
     sibling = remote(gram_all.at[core], gram_all.at[core], sems.at[6], sems.at[7], col=c + 1 - 2 * core)
     sibling.start()
+    spread.forward(4)
     sibling.wait_recv()
 
     def place_tiles(k, carry):
@@ -404,35 +419,21 @@
         return carry
 
     lax.fori_loop(0, COLS, place_tiles, 0)
-    spread = Gather(r, cross_all, cross_send, cross_recv)
-
     def factor_step(b, carry):
         def midway():
             @pl.when(b == 0)
             def _():
-                for h in range(2):
-                    cross_all[r, pl.ds(16 * h, 16), :] = reduce.end(h).astype(BF16)
-                spread.start()
-
-            @pl.when(b == 1)
-            def _():
-                spread.forward(2)
+                spread.forward(6)
 
         factor_rows(work, block, spare, b, midway)
-
-        @pl.when(b == 2)
-        def _():
-            spread.forward(4)
-
         return carry
 
     lax.fori_loop(0, 4, factor_step, 0)
-    spread.forward(6)
     for d in (1, 3, 5, 7, 8):
         spread.end(d)
 
     high, low_part = split(work[:512, 512:])
-    cross = cross_all[...].reshape(512, 896)
+    cross = jnp.concatenate([cross_all[8:], cross_all[:8]], axis=0).reshape(512, 896)
     right = jnp.dot(high, cross, preferred_element_type=F32) + jnp.dot(low_part, cross, preferred_element_type=F32)
     square_high, square_low = split(right * right)
     ones = jnp.ones((8, 896), BF16)

time: 107 us -> 98.5 us (0.921)
  Pallas kernels: 105 us -> 96.8 us
    pallas_call x1, Pallas kernels: 102 us -> 93.6 us  [main_call(): pl.pallas_call(main_kernel, out_shape=[jax.ShapeDtypeStruct((512, 512), B...]
where the time goes in v4:
time: 98.5 us; the launch traced here: 98.3 us
  Pallas kernels  96.8 us (98%)
    pallas_call x1, Pallas kernels, main_call(): pl.pallas_call(main_kernel, out_shape=[jax.ShapeDtypeStruct((512, 512), B...  93.6 us
    pallas_call x1, Pallas kernels, out_call(): pl.pallas_call(out_kernel, out_shape=[jax.ShapeDtypeStruct((512, 896), BF...  3.2 us

profile of v4, /device:TPU:1, one launch (start us, length us, event | category | flops | bytes accessed | tf_op | source)
XLA Modules:
  0.0 98.3 jit_solution(9243135111250144322)
XLA Ops:
  0.6 0.0 copy-start
  0.6 0.8 copy-done
  1.5 93.6 %shard_map.67 = (bf16[512,512]{1,0:T(8,128)(2,1)S(1)}, bf16[512,896]{1,0:T(8,128)(2,1)}, bf16[512,896]{1,0:T(8,128)(2,1)}, bf16[512,896]{1,0:T(8,128)(2,1)}) custom-call(bf16[32,896]{1,0:T(8,128)(2,1)S(1)} %bitcast.2, bf16[512,896]{1,0:T(8,128)(2,1)} %momentum.1, bf16[512,896]{1,0:T(8,128)(2,1)} %gradient.1, bf16[512,896]{1,0:T(8,128)(2,1)} %weight.1), custom_call_target="tpu_custom_call" | custom-call | tf_op jit(solution)/shard_map/pallas_call | solution.py:486
  95.1 3.2 %shard_map.68 = (bf16[512,896]{1,0:T(8,128)(2,1)}, bf16[512,896]{1,0:T(8,128)(2,1)}, bf16[32,896]{1,0:T(8,128)(2,1)}) custom-call(bf16[512,512]{1,0:T(8,128)(2,1)S(1)} %get-tuple-element.10.ortho, bf16[512,896]{1,0:T(8,128)(2,1)} %get-tuple-element.11.basis, bf16[512,896]{1,0:T(8,128)(2,1)} %get-tuple-element.12.momentum, ...), custom_call_target="tpu_custom_call" | custom-call | tf_op jit(solution)/shard_map/pallas_call | solution.py:549
Async XLA Ops:
  0.6 0.8 copy-start

commit v5 on v4

--- a/solution.py
+++ b/solution.py
@@ -13,7 +13,7 @@
 ROWS = 16
 COLS = 32
 TILES = 5
-LIMIT = 53 * 2**20
+LIMIT = 50 * 2**20
 F32 = jnp.float32
 BF16 = jnp.bfloat16
 MESH = pl.DeviceIdType.MESH

time: 98.5 us -> 95.5 us (0.970)
  Pallas kernels: 96.8 us -> 93.8 us
    pallas_call x1, Pallas kernels: 3.2 us -> 1.48 us  [out_call(): pl.pallas_call(out_kernel, out_shape=[jax.ShapeDtypeStruct((512, 896), BF...]
    pallas_call x1, Pallas kernels: 93.6 us -> 92.4 us  [main_call(): pl.pallas_call(main_kernel, out_shape=[jax.ShapeDtypeStruct((512, 512), B...]
where the time goes in v5:
time: 95.5 us; the launch traced here: 95.3 us
  Pallas kernels  93.8 us (98%)
    pallas_call x1, Pallas kernels, main_call(): pl.pallas_call(main_kernel, out_shape=[jax.ShapeDtypeStruct((512, 512), B...  92.4 us

profile of v5, /device:TPU:1, one launch (start us, length us, event | category | flops | bytes accessed | tf_op | source)
XLA Modules:
  0.0 95.3 jit_solution(18060399773269162618)
XLA Ops:
  0.6 0.0 copy-start
  0.6 0.8 copy-done
  1.5 92.4 %shard_map.67 = (bf16[512,512]{1,0:T(8,128)(2,1)S(1)}, bf16[512,896]{1,0:T(8,128)(2,1)S(1)}, bf16[512,896]{1,0:T(8,128)(2,1)S(1)}, bf16[512,896]{1,0:T(8,128)(2,1)S(1)}) custom-call(bf16[32,896]{1,0:T(8,128)(2,1)S(1)} %bitcast.2, bf16[512,896]{1,0:T(8,128)(2,1)} %momentum.1, bf16[512,896]{1,0:T(8,128)(2,1)} %gradient.1, bf16[512,896]{1,0:T(8,128)(2,1)} %weight.1), custom_call_target="tpu_custom_call" | custom-call | tf_op jit(solution)/shard_map/pallas_call | solution.py:486
  93.8 1.5 %shard_map.68 = (bf16[512,896]{1,0:T(8,128)(2,1)}, bf16[512,896]{1,0:T(8,128)(2,1)}, bf16[32,896]{1,0:T(8,128)(2,1)}) custom-call(bf16[512,512]{1,0:T(8,128)(2,1)S(1)} %get-tuple-element.10.ortho, bf16[512,896]{1,0:T(8,128)(2,1)S(1)} %get-tuple-element.11.basis, bf16[512,896]{1,0:T(8,128)(2,1)S(1)} %get-tuple-element.12.momentum, ...), custom_call_target="tpu_custom_call" | custom-call | tf_op jit(solution)/shard_map/pallas_call | solution.py:549
Async XLA Ops:
  0.6 0.8 copy-start
